TPU v7x, 512 devices: a whole 4x8x8 slice. The times are simulated.
512 devices in a mesh: gossip: 32 (over z, x_hi, core), fsdp: 16 (over x_lo, y).
Axes of the slice: x: 4 (x_hi: 2, x_lo: 2; x = x_hi * 2 + x_lo), y: 8, z: 8, core: 2. Of those that a mesh axis runs over, the one named last changes fastest.
Arguments:
- patches: bfloat16 [65536, 2048], P(('gossip', 'fsdp')), may hold values from -6 to 6
- query_weight: bfloat16 [32, 2048, 2048], P('gossip', 'fsdp'), may hold values from -6 to 6
- query_grad: bfloat16 [65536, 2048], P(('gossip', 'fsdp')), may hold values from -6 to 6
- step: int32 [1], replicated, may hold values from 0 to 63
Outputs:
- new_weight: bfloat16 [32, 2048, 2048], P('gossip', 'fsdp')
All inputs are finite; a program needn't handle non-finite values.
Results may differ from a plain program's by a relative error of at most 0.0056.
Values may be sent and summed in bfloat16 or wider, within the bound.
A program may use at most 64 MiB of HBM per device.

v0:
```python
from functools import partial

import jax
import jax.numpy as jnp
from jax import lax
from jax.sharding import PartitionSpec as P

DIN = 2048
HD = 128


epsilon = 1e-06


def for_sending(value):
    return jax.tree.map(lambda a: a.astype(jnp.bfloat16) if a.dtype == jnp.float32 else a, value)


def from_behind(value, axis, by):
    peers = lax.axis_size(axis)
    return lax.ppermute(value, axis, [(i, (i + by) % peers) for i in range(peers)])


def add_rows(patches, running, shard_part, first_row):
    return jnp.dot(patches, shard_part, preferred_element_type=jnp.float32)


def add_grads(patch_cols, shard_part):
    return lax.dot_general(
        patch_cols, shard_part, (((0,), (0,)), ((), ())), preferred_element_type=jnp.float32
    )


def head_norm_grad(proj, grad_part, proj_scale):
    tok_count = proj.shape[0]
    shaped = proj.reshape(tok_count, -1, HD)
    inv_rms = lax.rsqrt(jnp.mean(shaped * shaped, axis=-1, keepdims=True) + epsilon)
    normed = shaped * inv_rms
    cotangent = grad_part.astype(jnp.float32).reshape(shaped.shape)
    inner = jnp.mean(cotangent * normed, axis=-1, keepdims=True)
    grad_proj = proj_scale * inv_rms * (cotangent - normed * inner)
    return grad_proj.reshape(tok_count, -1).astype(jnp.bfloat16)


def partner_rows(updated, hop_size):
    if hop_size == 0:
        return updated
    return jax.tree.map(
        lambda part, own: part.astype(own.dtype),
        from_behind(for_sending(updated), "gossip", hop_size),
        updated,
    )


def exchange_columns(patches):
    return lax.all_to_all(patches, "fsdp", split_axis=1, concat_axis=0, tiled=True)


def on_device(patches, query_weight, query_grad, step):
    weight_rows = query_weight[0]
    tok_count = patches.shape[0]
    feat_count = weight_rows.shape[1]
    proj_scale = DIN ** (-0.5)
    fold_rows = partial(add_rows, patches)
    empty = jnp.zeros((tok_count, feat_count), jnp.float32)
    proj = (
        fold_rows(empty, lax.all_gather(weight_rows, "fsdp", axis=0, tiled=True), jnp.int32(0))
        * proj_scale
    )
    grad_proj = head_norm_grad(proj, query_grad, proj_scale)
    patch_cols = exchange_columns(patches)
    weight_grad = add_grads(patch_cols, lax.all_gather(grad_proj, "fsdp", axis=0, tiled=True))
    learn_rate = 0.5 + (step[0] % 64).astype(jnp.float32) / 64.0
    updated = (weight_rows.astype(jnp.float32) - learn_rate * weight_grad).astype(jnp.bfloat16)
    replica_count = lax.axis_size("gossip")
    branches = [
        partial(partner_rows, updated, 2**exponent % replica_count) for exponent in range(4)
    ]
    partner = lax.switch(step[0] % 4, branches)
    mixed = (updated.astype(jnp.float32) + partner.astype(jnp.float32)) * 0.5
    return mixed.astype(jnp.bfloat16)[None]


def solution(mesh):
    in_specs = (
        P(("gossip", "fsdp"), None),
        P("gossip", "fsdp", None),
        P(("gossip", "fsdp"), None),
        P(),
    )
    out_specs = P("gossip", "fsdp", None)
    return jax.shard_map(
        on_device, mesh=mesh, in_specs=in_specs, out_specs=out_specs, check_vma=False
    )
```

profile of v0, /device:TPU:24, one launch (start us, length us, event | category | flops | bytes accessed | tf_op | source)
XLA Modules:
  0.0 261.6 jit_solution(992021621953189534)
XLA Ops:
  6.5 0.0 all-gather.6.cloned.1.call-start
  6.5 0.7 all-gather.6.cloned.1.call-update
  7.3 0.0 all-gather.4.cloned.1.call-start
  7.3 1.1 convert_bitcast_fusion
  8.5 0.2 copy.31
  8.6 107.4 %all-gather.6.cloned.1.call-done = bf16[1,2048,2048]{2,1,0:T(8,128)(2,1)} async-done(((bf16[1,128,2048]{2,1,0:T(8,128)(2,1)}), bf16[1,2048,2048]{2,1,0:T(8,128)(2,1)}) %all-gather.6.cloned.1.call-update) | async-done | bytes 8388624 | tf_op jit(solution)/shard_map/all_gather | solution.py:67
  116.1 4.9 %fusion.3 = f32[128,2048]{1,0:T(8,128)S(1)} fusion(bf16[128,2048]{1,0:T(8,128)(2,1)} %param.8, bf16[1,2048,2048]{2,1,0:T(8,128)(2,1)} %all-gather.6.cloned.1.call-done), kind=kOutput, calls=%fused_computation.4 | convolution fusion | flops 1074003968 | bytes 9961472 | tf_op jit(solution)/shard_map/dot_general | solution.py:25
  121.0 0.0 copy-start.1
  121.0 0.0 copy-start
  121.0 0.0 copy-start.2
  121.0 0.2 copy.28
  121.2 0.3 multiply_reduce_fusion.1
  121.6 0.6 multiply_reduce_fusion
  122.2 0.3 mul.86
  122.5 0.3 mul.81
  122.9 0.3 mul.79
  123.2 0.0 copy-done.1
  123.2 1.8 fusion.9
  125.1 0.0 all-gather.4.cloned.1.call-update
  125.1 0.0 copy-done
  125.1 1.0 copy.20
  126.1 6.0 %all-to-all-start = ((bf16[128,16,128]{0,2,1:T(8,128)(2,1)}), bf16[128,16,128]{0,2,1:T(8,128)(2,1)S(1)}, u32[]{:S(2)}, u32[]{:S(2)}) async-start(bf16[128,16,128]{0,2,1:T(8,128)(2,1)} %bitcast.3), calls=%async_computation | async-start | bytes 1048576 | tf_op jit(solution)/shard_map/all_to_all | solution.py:56
  132.8 0.0 copy-done.2
  132.8 0.3 copy.19
  133.2 16.3 %all-to-all-done = bf16[128,16,128]{0,2,1:T(8,128)(2,1)S(1)} async-done(((bf16[128,16,128]{0,2,1:T(8,128)(2,1)}), bf16[128,16,128]{0,2,1:T(8,128)(2,1)S(1)}, u32[]{:S(2)}, u32[]{:S(2)}) %all-to-all-start) | async-done | bytes 524320 | tf_op jit(solution)/shard_map/all_to_all | solution.py:56
  149.5 0.3 copy.21
  149.8 81.8 %all-gather.4.cloned.1.call-done = bf16[2048,2048]{1,0:T(8,128)(2,1)} async-done(((bf16[128,2048]{1,0:T(8,128)(2,1)}), bf16[2048,2048]{1,0:T(8,128)(2,1)}) %all-gather.4.cloned.1.call-update) | async-done | bytes 8388624 | tf_op jit(solution)/shard_map/all_gather | solution.py:72
  231.6 5.8 %fusion.7 = bf16[128,2048]{0,1:T(8,128)(2,1)S(1)} fusion(bf16[2048,2048]{1,0:T(8,128)(2,1)} %all-gather.4.cloned.1.call-done, bf16[2048,128]{1,0:T(8,128)(2,1)S(1)} %bitcast.52, bf16[1,128,2048]{1,2,0:T(8,128)(2,1)S(1)} %copy.19, f32[]{:T(128)S(6)} %add.28), kind=kOutput, calls=%fused_computation.6 | convolution fusion | flops 1074790400 | bytes 9961476 | tf_op jit(solution)/shard_map/dot_general | solution.py:29
  237.4 0.2 copy.22
  237.6 14.6 %conditional.4 = (bf16[128,2048]{1,0:T(8,128)(2,1)}) conditional(s32[]{:T(128)} %clamp.3, bf16[128,2048]{1,0:T(8,128)(2,1)S(1)} %copy.22, bf16[128,2048]{1,0:T(8,128)(2,1)S(1)} %copy.22, bf16[128,2048]{1,0:T(8,128)(2,1)S(1)} %copy.22, bf16[128,2048]{1,0:T(8,128)(2,1)S(1)} %copy.22), branch_computations={%region_2.3_spmd, %region_3.4_spmd, %region_4.5_spmd, %region_5.6_... | conditional | bytes 2097200
  237.6 2.0 collective-permute-start
  239.6 12.6 %collective-permute-done = bf16[128,2048]{1,0:T(8,128)(2,1)} collective-permute-done((bf16[128,2048]{1,0:T(8,128)(2,1)S(1)}, bf16[128,2048]{1,0:T(8,128)(2,1)}, u32[]{:S(2)}, u32[]{:S(2)}) %collective-permute-start) | collective-permute-done | bytes 524320 | tf_op jit(solution)/shard_map/cond/branch_0_fun/ppermute | solution.py:21
  252.2 1.3 copy.26
  253.5 0.2 fusion.10
  253.7 1.0 copy.27
  (2 shorter events, 0.0 us)
Async XLA Ops:
  6.5 109.6 %all-gather.6.cloned.1.call-start = ((), (), s32[]{:S(2)}) async-start(), calls=%async_computation.2 | async-start | bytes 8912896 | tf_op jit(solution)/shard_map/all_gather | solution.py:67
  7.3 224.3 %all-gather.4.cloned.1.call-start = ((), (), s32[]{:S(2)}) async-start(), calls=%async_computation.1 | async-start | bytes 8912896 | tf_op jit(solution)/shard_map/all_gather | solution.py:72
  121.0 2.3 copy-start.1
  121.0 4.1 %copy-start = (bf16[128,2048]{1,0:T(8,128)(2,1)S(1)}, bf16[128,2048]{1,0:T(8,128)(2,1)}, u32[]{:S(2)}) copy-start(bf16[128,2048]{1,0:T(8,128)(2,1)} %param.8) | copy-start | bytes 1572868
  121.0 11.9 %copy-start.2 = (bf16[1,128,2048]{2,1,0:T(8,128)(2,1)S(1)}, bf16[1,128,2048]{2,1,0:T(8,128)(2,1)}, u32[]{:S(2)}) copy-start(bf16[1,128,2048]{2,1,0:T(8,128)(2,1)} %param.9) | copy-start | bytes 1572868
  126.1 23.4 %all-to-all-start = ((bf16[128,16,128]{0,2,1:T(8,128)(2,1)}), bf16[128,16,128]{0,2,1:T(8,128)(2,1)S(1)}, u32[]{:S(2)}, u32[]{:S(2)}) async-start(bf16[128,16,128]{0,2,1:T(8,128)(2,1)} %bitcast.3), calls=%async_computation | async-start | bytes 1048576 | tf_op jit(solution)/shard_map/all_to_all | solution.py:56
  237.6 14.6 %collective-permute-start = (bf16[128,2048]{1,0:T(8,128)(2,1)S(1)}, bf16[128,2048]{1,0:T(8,128)(2,1)}, u32[]{:S(2)}, u32[]{:S(2)}) collective-permute-start(bf16[128,2048]{1,0:T(8,128)(2,1)S(1)} %param), channel_id=1, source_target_pairs={{0,16},{16,32},{32,48},{48,64},{64,80},{80,96},{96,112},{112,128},... | collective-permute-start | bytes 1572872 | tf_op jit(solution)/shard_map/cond/branch_0_fun/ppermute | solution.py:21
Sparse Core Ops, SparseCore 0:
  9.4 106.6 all-gather.5
  125.2 106.3 all-gather.3
where the time goes:
time: 262 us
  waiting for transfers between devices  219 us (84%)
  between operations  14.2 us (5%)
  matrix products  10.6 us (4%)
  starting transfers between devices  8.05 us (3%)
  local copies, waits for them, and re-layouts  5.51 us (2%)
  other arithmetic  4.16 us (2%)
    all_gather x1, waiting for transfers between devices, on_device(): lax.all_gather(weight_rows, 'fsdp', axis=0, tiled=True)  107 us
    all_gather x1, waiting for transfers between devices, on_device(): lax.all_gather(grad_proj, 'fsdp', axis=0, tiled=True)  81.8 us
    all_to_all x1, waiting for transfers between devices, exchange_columns(): lax.all_to_all(patches, 'fsdp', split_axis=1, concat_axis=0, tiled=True)  16.3 us
    ppermute x1, waiting for transfers between devices, from_behind(): lax.ppermute(value, axis, [(i, (i + by) % peers) for i in range(peers)])  12.6 us
    all_to_all x1, starting transfers between devices, exchange_columns(): lax.all_to_all(patches, 'fsdp', split_axis=1, concat_axis=0, tiled=True)  6.05 us
    dot_general x1, matrix products, add_grads(): lax.dot_general(patch_cols, shard_part, (((0,), (0,)), ((), ())), preferr...  5.78 us
  transfers between devices with their start and end apart: 4, of which 4 were waited for; matrix products, arithmetic and copies ran while one was open for 1% of the time, Pallas kernels for 0%

commit v1 on v0

v1 whole, which is shorter than its diff:
```python
from functools import partial

import jax
import jax.numpy as jnp
from jax import lax
from jax.experimental import pallas as pl
from jax.experimental.pallas import tpu as pltpu
from jax.sharding import PartitionSpec as P

DIN = 2048
HQ = 2048
HD = 128
EPS = 1e-06
MESH = pl.DeviceIdType.MESH

NY = 8
ROWS = 128
FEATS = HQ // NY
HEADS = FEATS // HD
HALF = DIN // 2
TOKS = NY * ROWS
PIECES = 4
PROWS = ROWS // PIECES


def kernel(hop, lr_ref, p_in, w_in, q_in, out, pat, pat_t, wcol, grad_in, normed, scaled_inv, grad, own,
           rs_out, rs_in, upd, upd_in, mixed, loc, w_ss, w_rs, wx_ss, wx_rs, ag_ss, ag_rs, q_ss, q_rs,
           rs_ss, rs_rs, g_ss, g_rs, o_ss, o_rs):
    replicas = lax.axis_size("gossip")
    g, f = lax.axis_index("gossip"), lax.axis_index("fsdp")
    x, y = f // NY, f % NY

    def ring(d):
        return (y + d + NY) % NY

    def along_y(d):
        return (g, x * NY + ring(d))

    across = (g, (1 - x) * NY + y)
    ahead = ((g + hop) % replicas, f)
    behind = ((g + replicas - hop) % replicas, f)

    def copy(src, dst, ss, rs, to):
        return pltpu.make_async_remote_copy(
            src_ref=src, dst_ref=dst, send_sem=ss, recv_sem=rs, device_id=to, device_id_type=MESH)

    def arrived(dst, ss, rs):
        copy(dst, dst, ss, rs, across).wait_recv()

    def block(i, size):
        return pl.ds(pl.multiple_of(i * size, size), size)

    barrier = pltpu.get_barrier_semaphore()
    peers = [along_y(d) for d in range(1, NY)] + [across, ahead, behind]
    for peer in peers:
        pl.semaphore_signal(barrier, inc=1, device_id=peer, device_id_type=MESH)

    cols = block(y, FEATS)
    mine = wcol.at[block(f, ROWS), :]
    local = [
        pltpu.make_async_copy(p_in, pat.at[0], loc.at[0]),
        pltpu.make_async_copy(w_in.at[0, :, cols], mine, loc.at[1]),
    ] + [
        pltpu.make_async_copy(q_in.at[:, block(y * HEADS + h, HD)], grad_in.at[h, 0], loc.at[2 + h])
        for h in range(HEADS)
    ]
    for c in local:
        c.start()
    pl.semaphore_wait(barrier, len(peers))

    sent = []

    def send(*a):
        c = copy(*a)
        c.start()
        sent.append(c)

    for d in (4, 3, 5, 2, 6, 1, 7):
        send(w_in.at[0, :, block(ring(d), FEATS)], mine, w_ss.at[d], w_rs.at[d], along_y(d))
    send(w_in.at[0, :, cols], mine, wx_ss.at[0], wx_rs.at[0], across)

    def piece(ref, p):
        return ref.at[pl.ds(p * PROWS, PROWS), :]

    def on_ring(way, step, p):
        return step < NY // 2 or (p < PIECES // 2) == (way == 0)

    def push(way, step, p):
        slot = NY - step if way == 0 else step
        src = p_in if step == 1 else pat.at[slot + 1 if way == 0 else slot - 1]
        send(piece(src, p), piece(pat.at[slot], p), ag_ss.at[way, step, p], ag_rs.at[way, step, p],
             along_y(1 if way == 0 else -1))

    def pass_on(step):
        for p in range(PIECES):
            for way in range(2):
                if not on_ring(way, step, p):
                    continue
                slot = NY - step if way == 0 else step
                arrived(piece(pat.at[slot], p), ag_ss.at[way, step, p], ag_rs.at[way, step, p])
                if step < NY // 2 and on_ring(way, step + 1, p):
                    push(way, step + 1, p)

    for p in range(PIECES):
        for way in range(2):
            push(way, 1, p)

    for d in (4, 3, 5, 2, 6, 1, 7):
        rows = wcol.at[block(x * NY + ring(-d), ROWS), :]
        arrived(rows, w_ss.at[d], w_rs.at[d])
        send(rows, rows, wx_ss.at[d], wx_rs.at[d], across)

    scale = DIN ** (-0.5)

    def turn(slot):
        pat_t[:, slot * ROWS:(slot + 1) * ROWS] = pat[slot].T

    def project(slot):
        proj = jnp.dot(pat[slot], wcol[...], preferred_element_type=jnp.float32) * scale
        rows = pl.ds(slot * ROWS, ROWS)
        for h in range(HEADS):
            part = proj[:, h * HD:(h + 1) * HD]
            inv = lax.rsqrt(jnp.mean(part * part, axis=-1, keepdims=True) + EPS)
            normed[h, rows, :] = part * inv
            scaled_inv[h, rows, :] = jnp.broadcast_to(scale * inv, part.shape)

    for c in local:
        c.wait()
    pass_on(1)
    for s in (0, 7, 1):
        turn(s)
    pass_on(2)
    for d in range(NY):
        arrived(wcol.at[block((1 - x) * NY + ring(-d), ROWS), :], wx_ss.at[d], wx_rs.at[d])
    for s in (6, 2):
        turn(s)
    for s in (0, 7, 1, 6, 2):
        project(s)
    pass_on(3)
    for h in range(HEADS):
        for d in (4, 3, 5, 2, 6, 1, 7):
            send(q_in.at[:, block(ring(d) * HEADS + h, HD)], grad_in.at[h, NY - d],
                 q_ss.at[h, d], q_rs.at[h, d], along_y(d))
    for s in (5, 3):
        turn(s)
        project(s)
    pass_on(4)
    turn(4)
    project(4)

    rate = lr_ref[0]

    def weight_grad(half, i, h):
        rows = block(half * NY + ring(i + 1), ROWS)
        return jnp.dot(pat_t[rows, :], grad[h], preferred_element_type=jnp.float32)

    def gradient(h):
        for d in range(1, NY):
            arrived(grad_in.at[h, NY - d], q_ss.at[h, d], q_rs.at[h, d])
        cot = grad_in[h].astype(jnp.float32).reshape(TOKS, HD)
        norm = normed[h]
        inner = jnp.mean(cot * norm, axis=-1, keepdims=True)
        grad[h] = (scaled_inv[h] * (cot - norm * inner)).astype(jnp.bfloat16)

        @pl.loop(0, NY)
        def _(i):
            rs_out[h, i] = weight_grad(1 - x, i, h).astype(jnp.bfloat16)
            copy(rs_out.at[h, i], rs_in.at[h, i], rs_ss.at[h, i], rs_rs.at[h, i], across).start()

        @pl.loop(0, NY)
        def _(i):
            own[h, i] = weight_grad(x, i, h)

    def update(h):
        @pl.loop(0, NY)
        def _(i):
            arrived(rs_in.at[h, i], rs_ss.at[h, i], rs_rs.at[h, i])
            total = own[h, i] + rs_in[h, i].astype(jnp.float32)
            old = wcol[block(x * NY + ring(i + 1), ROWS), h * HD:(h + 1) * HD].astype(jnp.float32)
            upd[h, i] = (old - rate * total).astype(jnp.bfloat16)
            copy(upd.at[h, i], upd_in.at[h, i], g_ss.at[h, i], g_rs.at[h, i], ahead).start()

    def place(d, h):
        return out.at[0, :, block(ring(d) * HEADS + h, HD)]

    def mix(h):
        def average(i):
            arrived(upd_in.at[h, i], g_ss.at[h, i], g_rs.at[h, i])
            mean = (upd[h, i].astype(jnp.float32) + upd_in[h, i].astype(jnp.float32)) * 0.5
            mixed[h, i] = mean.astype(jnp.bfloat16)

        @pl.loop(0, NY - 1)
        def _(i):
            average(i)
            copy(mixed.at[h, i], place(0, h), o_ss.at[h, i], o_rs.at[h, i], along_y(i + 1)).start()

        average(NY - 1)
        pltpu.make_async_copy(mixed.at[h, NY - 1], place(0, h), loc.at[h]).start()

    gradient(0)
    update(0)
    gradient(1)
    mix(0)
    update(1)
    mix(1)

    for c in sent:
        c.wait_send()
    for h in range(HEADS):
        pltpu.make_async_copy(mixed.at[h, NY - 1], place(0, h), loc.at[h]).wait()

        @pl.loop(0, NY)
        def _(i):
            copy(rs_out.at[h, i], rs_in.at[h, i], rs_ss.at[h, i], rs_rs.at[h, i], across).wait_send()
            copy(upd.at[h, i], upd_in.at[h, i], g_ss.at[h, i], g_rs.at[h, i], ahead).wait_send()

        @pl.loop(0, NY - 1)
        def _(i):
            copy(mixed.at[h, i], place(0, h), o_ss.at[h, i], o_rs.at[h, i], along_y(i + 1)).wait_send()
            arrived(place(-(i + 1), h), o_ss.at[h, i], o_rs.at[h, i])


def update_weights(exponent, rate, patches, weight, query_grad):
    bf16, f32 = jnp.bfloat16, jnp.float32
    dma = pltpu.SemaphoreType.DMA
    blocks = (HEADS, NY, ROWS, HD)
    return pl.pallas_call(
        partial(kernel, 2 ** exponent),
        out_shape=jax.ShapeDtypeStruct(weight.shape, bf16),
        in_specs=[pl.BlockSpec(memory_space=pltpu.SMEM)] + [pl.BlockSpec(memory_space=pl.ANY)] * 3,
        out_specs=pl.BlockSpec(memory_space=pl.ANY),
        scratch_shapes=[
            pltpu.VMEM((NY, ROWS, DIN), bf16),
            pltpu.VMEM((DIN, TOKS), bf16),
            pltpu.VMEM((DIN, FEATS), bf16),
            pltpu.VMEM(blocks, bf16),
            pltpu.VMEM((HEADS, TOKS, HD), f32),
            pltpu.VMEM((HEADS, TOKS, HD), f32),
            pltpu.VMEM((HEADS, TOKS, HD), bf16),
            pltpu.VMEM(blocks, f32),
            pltpu.VMEM(blocks, bf16),
            pltpu.VMEM(blocks, bf16),
            pltpu.VMEM(blocks, bf16),
            pltpu.VMEM(blocks, bf16),
            pltpu.VMEM(blocks, bf16),
            dma((4,)),
            dma((NY,)), dma((NY,)),
            dma((NY,)), dma((NY,)),
            dma((2, NY // 2 + 1, PIECES)), dma((2, NY // 2 + 1, PIECES)),
            dma((HEADS, NY)), dma((HEADS, NY)),
            dma((HEADS, NY)), dma((HEADS, NY)),
            dma((HEADS, NY)), dma((HEADS, NY)),
            dma((HEADS, NY)), dma((HEADS, NY)),
        ],
        compiler_params=pltpu.CompilerParams(
            collective_id=exponent, has_side_effects=True, vmem_limit_bytes=40 << 20),
        cost_estimate=pl.CostEstimate(
            flops=8 * TOKS * DIN * FEATS, bytes_accessed=8 << 20, transcendentals=TOKS * HEADS),
        name=f"replica_update_hop{2 ** exponent}",
    )(rate, patches, weight, query_grad)


def on_device(patches, query_weight, query_grad, step):
    rate = 0.5 + (step % 64).astype(jnp.float32) / 64.0
    branches = [partial(update_weights, exponent) for exponent in range(4)]
    return lax.switch(step[0] % 4, branches, rate, patches, query_weight, query_grad)


def solution(mesh):
    in_specs = (
        P(("gossip", "fsdp"), None),
        P("gossip", "fsdp", None),
        P(("gossip", "fsdp"), None),
        P(),
    )
    out_specs = P("gossip", "fsdp", None)
    return jax.shard_map(
        on_device, mesh=mesh, in_specs=in_specs, out_specs=out_specs, check_vma=False
    )
```

time: 262 us -> 100 us (0.38)
  the two profiles are of different devices: /device:TPU:24 before, /device:TPU:2 now
where the time goes in v1:
time: 100 us
  Pallas kernels  98.3 us (98%)
    pallas_call x1, Pallas kernels, update_weights(): pl.pallas_call(partial(kernel, 2 ** exponent), out_shape=jax.ShapeDtypeSt...  98.3 us

profile of v1, /device:TPU:2, one launch (start us, length us, event | category | flops | bytes accessed | tf_op | source)
XLA Modules:
  0.0 100.2 jit_solution(14813114950969843696)
XLA Ops:
  0.7 98.7 %conditional.1 = (bf16[1,128,2048]{2,1,0:T(8,128)(2,1)S(1)}) conditional(s32[]{:T(128)} %clamp.3, (f32[1]{0:T(128)}, bf16[128,2048]{1,0:T(8,128)(2,1)}, bf16[1,128,2048]{2,1,0:T(8,128)(2,1)}, bf16[128,2048]{1,0:T(8,128)(2,1)}) %tuple.41, (f32[1]{0:T(128)}, bf16[128,2048]{1,0:T(8,128)(2,1)}, ...), branch_computations={%region_0.1_spmd.clone, %region_1.2_spmd.clone, %region_2.3_spmd.c... | conditional | flops 4294967296 | bytes 8388640 | solution.py:266
  0.9 98.3 %replica_update_hop4.1 = bf16[1,128,2048]{2,1,0:T(8,128)(2,1)S(1)} custom-call(f32[1]{0:T(128)S(6)} %add.22.lr_ref, bf16[128,2048]{1,0:T(8,128)(2,1)} %get-tuple-element.116.p_in, bf16[1,128,2048]{2,1,0:T(8,128)(2,1)} %get-tuple-element.117.w_in, bf16[128,2048]{1,0:T(8,128)(2,1)} %get-tuple-element.118.q_in), custom_call_target="tpu_custom_call" | custom-call | flops 4294967296 | bytes 8388608 | tf_op jit(solution)/shard_map/cond/branch_2_fun/replica_update_hop4/pallas_call | solution.py:227
  99.4 0.8 copy.43

commit v2 on v1

v2 whole, which is shorter than its diff:
```python
from functools import partial

import jax
import jax.numpy as jnp
from jax import lax
from jax.experimental import pallas as pl
from jax.experimental.pallas import tpu as pltpu
from jax.sharding import PartitionSpec as P

DIN = 2048
HQ = 2048
HD = 128
EPS = 1e-06
MESH = pl.DeviceIdType.MESH

NY = 8
ROWS = 128
HALF = DIN // 2
FEATS = HQ // (NY // 2)
HEADS = FEATS // HD
SLOTS = 4
TOKS = 2 * SLOTS * ROWS
PIECES = 4
PROWS = 2 * ROWS // PIECES
OTHER_FIRST = (2, 3, 0, 1)


def kernel(hop, lr_ref, p_in, w_in, q_in, out, pat, pat_t, wcol, part, part_out, part_in, grad_in, normed,
           scaled_inv, grad, own, rs_out, rs_in, upd, upd_in, mixed, loc, pre_ss, pre_rs, w_ss, w_rs, ag_ss, ag_rs,
           pt_ss, pt_rs, q_ss, q_rs, x_ss, x_rs, rs_ss, rs_rs, g_ss, g_rs, o_ss, o_rs):
    replicas = lax.axis_size("gossip")
    g, f = lax.axis_index("gossip"), lax.axis_index("fsdp")
    x, y = f // NY, f % NY
    sign = 1 - 2 * (y % 2)

    def ring(k):
        return (y + k * sign + NY) % NY

    def node(k):
        return (g, x * NY + ring(k))

    def pair(k):
        return ring(k) // 2

    across = (g, (1 - x) * NY + y)
    ahead = ((g + hop) % replicas, f)
    behind = ((g + replicas - hop) % replicas, f)

    def copy(src, dst, ss, rs, to):
        return pltpu.make_async_remote_copy(
            src_ref=src, dst_ref=dst, send_sem=ss, recv_sem=rs, device_id=to, device_id_type=MESH)

    def arrived(dst, ss, rs):
        copy(dst, dst, ss, rs, across).wait_recv()

    def block(i, size):
        return pl.ds(pl.multiple_of(i * size, size), size)

    barrier = pltpu.get_barrier_semaphore()
    peers = [node(k) for k in (1, -1, 2, -2, -3)] + [across, ahead, behind]
    for peer in peers:
        pl.semaphore_signal(barrier, inc=1, device_id=peer, device_id_type=MESH)

    def head_cols(k, h):
        return block(pair(k) * HEADS + h, HD)

    def weight_rows(k):
        return wcol.at[block(ring(k), ROWS), :]

    local = [
        pltpu.make_async_copy(p_in.at[:, block(x, HALF)], pat.at[0, 0], loc.at[0]),
        pltpu.make_async_copy(w_in.at[0, :, block(pair(0), FEATS)], weight_rows(0), loc.at[1]),
    ] + [
        pltpu.make_async_copy(q_in.at[:, head_cols(0, h)], grad_in.at[h, 0], loc.at[2 + h]) for h in range(HEADS)
    ]
    for c in local:
        c.start()
    pl.semaphore_wait(barrier, len(peers))

    sent = []

    def send(*a):
        c = copy(*a)
        c.start()
        sent.append(c)

    for p in range(PIECES // 2):
        rows = pl.ds(p * PROWS, PROWS)
        send(p_in.at[rows, block(1 - x, HALF)], pat.at[0, 1, rows, :], pre_ss.at[p], pre_rs.at[p], across)

    def piece(slot, p):
        return pat.at[slot, p // 2, pl.ds(p % 2 * PROWS, PROWS), :]

    def push(src, slot, p, to):
        send(src, piece(slot, p), ag_ss.at[slot, p], ag_rs.at[slot, p], node(to))

    def landed(slot, p):
        arrived(piece(slot, p), ag_ss.at[slot, p], ag_rs.at[slot, p])

    for k, sem in ((-3, 3), (2, 2), (-1, 1), (1, 0)):
        send(w_in.at[0, :, block(pair(k), FEATS)], weight_rows(0), w_ss.at[sem], w_rs.at[sem], node(k))
    for p in OTHER_FIRST:
        src = piece(0, p)
        if p < PIECES // 2:
            src = p_in.at[pl.ds(p * PROWS, PROWS), block(x, HALF)]
        else:
            q = p - PIECES // 2
            arrived(src, pre_ss.at[q], pre_rs.at[q])
        push(src, 1, p, -1)
        push(src, 4, p, 1)
    for k in (1, 2, 3):
        arrived(weight_rows(-k), w_ss.at[k], w_rs.at[k])
        send(weight_rows(-k), weight_rows(-k), w_ss.at[3 + k], w_rs.at[3 + k], node(1))

    def send_grads(h):
        for k, sem in ((-3, 3), (2, 2), (-1, 1)):
            send(q_in.at[:, head_cols(k, h)], grad_in.at[h, sem], q_ss.at[h, sem], q_rs.at[h, sem], node(k))

    scale = DIN ** (-0.5)

    def turn(slot):
        for c in range(2):
            at = (c * SLOTS + slot) * ROWS
            pat_t[:, at:at + ROWS] = pat[slot, c].T

    def product(slot, c):
        return jnp.dot(pat[slot, c], wcol[...], preferred_element_type=jnp.float32)

    def project_other(slot):
        part_out[slot] = product(slot, 1).astype(jnp.bfloat16)
        send(part_out.at[slot], part_in.at[slot], pt_ss.at[slot], pt_rs.at[slot], across)

    def project_own(slot):
        part[slot] = product(slot, 0)

    def project(slot):
        project_other(slot)
        project_own(slot)

    def finish(slot):
        arrived(part_in.at[slot], pt_ss.at[slot], pt_rs.at[slot])
        proj = (part[slot] + part_in[slot].astype(jnp.float32)) * scale
        rows = pl.ds(slot * ROWS, ROWS)
        for h in range(HEADS):
            own_part = proj[:, h * HD:(h + 1) * HD]
            inv = lax.rsqrt(jnp.mean(own_part * own_part, axis=-1, keepdims=True) + EPS)
            normed[h, rows, :] = own_part * inv
            scaled_inv[h, rows, :] = jnp.broadcast_to(scale * inv, own_part.shape)

    for c in local:
        c.wait()
    turn(0)
    for p in OTHER_FIRST:
        landed(1, p)
        push(piece(1, p), 5, p, 1)
        landed(4, p)
        push(piece(4, p), 2, p, -1)
    turn(1)
    arrived(weight_rows(1), w_ss.at[0], w_rs.at[0])
    for k in (1, 2, 3):
        arrived(weight_rows(k + 1), w_ss.at[3 + k], w_rs.at[3 + k])
    project(0)
    project(1)
    for p in OTHER_FIRST:
        landed(5, p)
        push(piece(5, p), 3, p, -1)
        landed(2, p)
    turn(2)
    project(2)
    finish(0)
    finish(1)
    early = len(sent)
    for p in OTHER_FIRST:
        landed(3, p)
        for h in GRADS_AT[p]:
            send_grads(h)
        if p == OTHER_FIRST[1]:
            project_other(3)
            for c in sent[:early]:
                c.wait_send()
            finish(2)
    project_own(3)
    turn(3)
    finish(3)

    rate = lr_ref[0]

    def grad_across(h, slot):
        return copy(grad.at[h, pl.ds(slot * ROWS, ROWS), :], grad.at[h, pl.ds((SLOTS + slot) * ROWS, ROWS), :],
                    x_ss.at[h, slot], x_rs.at[h, slot], across)

    def to_pair(h, i):
        return copy(rs_out.at[h, i], rs_in.at[h, i], rs_ss.at[h, i], rs_rs.at[h, i], node(1))

    def to_partner(h, i):
        return copy(upd.at[h, i], upd_in.at[h, i], g_ss.at[h, i], g_rs.at[h, i], ahead)

    def to_owner(h, i):
        place = out.at[0, :, head_cols(0, h)]
        if i == 0:
            return pltpu.make_async_copy(mixed.at[h, i], place, loc.at[h])
        return copy(mixed.at[h, i], place, o_ss.at[h, i], o_rs.at[h, i], node(-i))

    def gradient(h):
        for slot in range(SLOTS):
            if slot:
                arrived(grad_in.at[h, slot], q_ss.at[h, slot], q_rs.at[h, slot])
            rows = pl.ds(slot * ROWS, ROWS)
            cot = grad_in[h, slot].astype(jnp.float32)
            norm = normed[h, rows, :]
            inner = jnp.mean(cot * norm, axis=-1, keepdims=True)
            grad[h, rows, :] = (scaled_inv[h, rows, :] * (cot - norm * inner)).astype(jnp.bfloat16)
            grad_across(h, slot).start()

    def weight_grad(k, h):
        return jnp.dot(pat_t[block(ring(k), ROWS), :], grad[h], preferred_element_type=jnp.float32)

    def sums(h):
        for slot in range(SLOTS):
            arrived(grad.at[h, pl.ds((SLOTS + slot) * ROWS, ROWS), :], x_ss.at[h, slot], x_rs.at[h, slot])
        for i in range(SLOTS):
            rs_out[h, i] = weight_grad(i + 1, h).astype(jnp.bfloat16)
            to_pair(h, i).start()
        for i in range(SLOTS):
            own[h, i] = weight_grad(-i, h)

    def update(h):
        for i in range(SLOTS):
            arrived(rs_in.at[h, i], rs_ss.at[h, i], rs_rs.at[h, i])
            total = own[h, i] + rs_in[h, i].astype(jnp.float32)
            old = wcol[block(ring(-i), ROWS), h * HD:(h + 1) * HD].astype(jnp.float32)
            upd[h, i] = (old - rate * total).astype(jnp.bfloat16)
            to_partner(h, i).start()

    def mix(h):
        for i in range(SLOTS):
            arrived(upd_in.at[h, i], g_ss.at[h, i], g_rs.at[h, i])
            mean = (upd[h, i].astype(jnp.float32) + upd_in[h, i].astype(jnp.float32)) * 0.5
            mixed[h, i] = mean.astype(jnp.bfloat16)
            to_owner(h, i).start()

    for step, h in STEPS:
        (gradient, sums, update, mix)[step](h)

    for c in sent[early:]:
        c.wait_send()
    for h in range(HEADS):
        for i in range(SLOTS):
            grad_across(h, i).wait_send()
            to_pair(h, i).wait_send()
            to_partner(h, i).wait_send()
            if i == 0:
                to_owner(h, i).wait()
            else:
                to_owner(h, i).wait_send()
                source = (None, -1, 2, -3)[i]
                arrived(out.at[0, :, head_cols(source, h)], o_ss.at[h, i], o_rs.at[h, i])


STEPS = ((0, 0), (0, 1), (1, 0), (0, 2), (1, 1), (2, 0), (0, 3), (1, 2), (2, 1), (3, 0), (1, 3), (2, 2), (3, 1),
         (2, 3), (3, 2), (3, 3))
GRADS_AT = ((1,2), (3,), (0,), ())


def update_weights(exponent, rate, patches, weight, query_grad):
    bf16, f32 = jnp.bfloat16, jnp.float32
    dma = pltpu.SemaphoreType.DMA
    blocks = (HEADS, SLOTS, ROWS, HD)
    return pl.pallas_call(
        partial(kernel, 2 ** exponent),
        out_shape=jax.ShapeDtypeStruct(weight.shape, bf16),
        in_specs=[pl.BlockSpec(memory_space=pltpu.SMEM)] + [pl.BlockSpec(memory_space=pl.ANY)] * 3,
        out_specs=pl.BlockSpec(memory_space=pl.ANY),
        scratch_shapes=[
            pltpu.VMEM((SLOTS + 2, 2, ROWS, HALF), bf16),
            pltpu.VMEM((HALF, TOKS), bf16),
            pltpu.VMEM((HALF, FEATS), bf16),
            pltpu.VMEM((SLOTS, ROWS, FEATS), f32),
            pltpu.VMEM((SLOTS, ROWS, FEATS), bf16),
            pltpu.VMEM((SLOTS, ROWS, FEATS), bf16),
            pltpu.VMEM(blocks, bf16),
            pltpu.VMEM((HEADS, SLOTS * ROWS, HD), f32),
            pltpu.VMEM((HEADS, SLOTS * ROWS, HD), f32),
            pltpu.VMEM((HEADS, TOKS, HD), bf16),
            pltpu.VMEM(blocks, f32),
            pltpu.VMEM(blocks, bf16),
            pltpu.VMEM(blocks, bf16),
            pltpu.VMEM(blocks, bf16),
            pltpu.VMEM(blocks, bf16),
            pltpu.VMEM(blocks, bf16),
            dma((2 + HEADS,)),
            dma((PIECES // 2,)), dma((PIECES // 2,)),
            dma((7,)), dma((7,)),
            dma((SLOTS + 2, PIECES)), dma((SLOTS + 2, PIECES)),
            dma((SLOTS,)), dma((SLOTS,)),
            dma((HEADS, SLOTS)), dma((HEADS, SLOTS)),
            dma((HEADS, SLOTS)), dma((HEADS, SLOTS)),
            dma((HEADS, SLOTS)), dma((HEADS, SLOTS)),
            dma((HEADS, SLOTS)), dma((HEADS, SLOTS)),
            dma((HEADS, SLOTS)), dma((HEADS, SLOTS)),
        ],
        compiler_params=pltpu.CompilerParams(
            collective_id=exponent, has_side_effects=True, vmem_limit_bytes=40 << 20),
        cost_estimate=pl.CostEstimate(
            flops=8 * TOKS * HALF * FEATS, bytes_accessed=8 << 20, transcendentals=SLOTS * ROWS * HEADS),
        name=f"replica_update_hop{2 ** exponent}",
    )(rate, patches, weight, query_grad)


def on_device(patches, query_weight, query_grad, step):
    rate = 0.5 + (step % 64).astype(jnp.float32) / 64.0
    branches = [partial(update_weights, exponent) for exponent in range(4)]
    return lax.switch(step[0] % 4, branches, rate, patches, query_weight, query_grad)


def solution(mesh):
    in_specs = (
        P(("gossip", "fsdp"), None),
        P("gossip", "fsdp", None),
        P(("gossip", "fsdp"), None),
        P(),
    )
    out_specs = P("gossip", "fsdp", None)
    return jax.shard_map(
        on_device, mesh=mesh, in_specs=in_specs, out_specs=out_specs, check_vma=False
    )
```

time: 100 us -> 106 us (1.060)
  the two profiles are of different devices: /device:TPU:2 before, /device:TPU:8 now
where the time goes in v2:
time: 106 us
  Pallas kernels  103 us (97%)
    pallas_call x1, Pallas kernels, update_weights(): pl.pallas_call(partial(kernel, 2 ** exponent), out_shape=jax.ShapeDtypeSt...  103 us

profile of v2, /device:TPU:8, one launch (start us, length us, event | category | flops | bytes accessed | tf_op | source)
XLA Modules:
  0.0 105.6 jit_solution(18298639839691484380)
XLA Ops:
  0.7 104.1 %conditional.1 = (bf16[1,128,2048]{2,1,0:T(8,128)(2,1)S(1)}) conditional(s32[]{:T(128)} %clamp.3, (f32[1]{0:T(128)}, bf16[128,2048]{1,0:T(8,128)(2,1)}, bf16[1,128,2048]{2,1,0:T(8,128)(2,1)}, bf16[128,2048]{1,0:T(8,128)(2,1)}) %tuple.41, (f32[1]{0:T(128)}, bf16[128,2048]{1,0:T(8,128)(2,1)}, ...), branch_computations={%region_0.1_spmd.clone, %region_1.2_spmd.clone, %region_2.3_spmd.c... | conditional | flops 4294967296 | bytes 8388640 | solution.py:313
  1.2 103.2 %replica_update_hop8.1 = bf16[1,128,2048]{2,1,0:T(8,128)(2,1)S(1)} custom-call(f32[1]{0:T(128)S(6)} %add.23.lr_ref, bf16[128,2048]{1,0:T(8,128)(2,1)} %get-tuple-element.124.p_in, bf16[1,128,2048]{2,1,0:T(8,128)(2,1)} %get-tuple-element.125.w_in, bf16[128,2048]{1,0:T(8,128)(2,1)} %get-tuple-element.126.q_in), custom_call_target="tpu_custom_call" | custom-call | flops 4294967296 | bytes 8388608 | tf_op jit(solution)/shard_map/cond/branch_3_fun/replica_update_hop8/pallas_call | solution.py:269
  104.8 0.8 copy.43

commit v3 on v2

--- a/solution.py
+++ b/solution.py
@@ -151,10 +151,10 @@
         c.wait()
     turn(0)
     for p in OTHER_FIRST:
+        landed(4, p)
+        push(piece(4, p), 2, p, -1)
         landed(1, p)
         push(piece(1, p), 5, p, 1)
-        landed(4, p)
-        push(piece(4, p), 2, p, -1)
     turn(1)
     arrived(weight_rows(1), w_ss.at[0], w_rs.at[0])
     for k in (1, 2, 3):

time: 106 us -> 105 us (level)
  the two profiles are of different devices: /device:TPU:8 before, /device:TPU:24 now
where the time goes in v3:
time: 105 us
  Pallas kernels  103 us (98%)
    pallas_call x1, Pallas kernels, update_weights(): pl.pallas_call(partial(kernel, 2 ** exponent), out_shape=jax.ShapeDtypeSt...  103 us

profile of v3, /device:TPU:24, one launch (start us, length us, event | category | flops | bytes accessed | tf_op | source)
XLA Modules:
  0.0 104.8 jit_solution(3976512604057757258)
XLA Ops:
  0.7 103.3 %conditional.1 = (bf16[1,128,2048]{2,1,0:T(8,128)(2,1)S(1)}) conditional(s32[]{:T(128)} %clamp.3, (f32[1]{0:T(128)}, bf16[128,2048]{1,0:T(8,128)(2,1)}, bf16[1,128,2048]{2,1,0:T(8,128)(2,1)}, bf16[128,2048]{1,0:T(8,128)(2,1)}) %tuple.41, (f32[1]{0:T(128)}, bf16[128,2048]{1,0:T(8,128)(2,1)}, ...), branch_computations={%region_0.1_spmd.clone, %region_1.2_spmd.clone, %region_2.3_spmd.c... | conditional | flops 4294967296 | bytes 8388640 | solution.py:313
  0.9 102.6 %replica_update_hop2.1 = bf16[1,128,2048]{2,1,0:T(8,128)(2,1)S(1)} custom-call(f32[1]{0:T(128)S(6)} %add.21.lr_ref, bf16[128,2048]{1,0:T(8,128)(2,1)} %get-tuple-element.108.p_in, bf16[1,128,2048]{2,1,0:T(8,128)(2,1)} %get-tuple-element.109.w_in, bf16[128,2048]{1,0:T(8,128)(2,1)} %get-tuple-element.110.q_in), custom_call_target="tpu_custom_call" | custom-call | flops 4294967296 | bytes 8388608 | tf_op jit(solution)/shard_map/cond/branch_1_fun/replica_update_hop2/pallas_call | solution.py:269
  104.0 0.8 copy.43
